TPU v7x, 32 devices: a whole 2x2x4 slice. The times are simulated.
32 devices in a mesh: phase: 4 (over x, core), seq: 8 (over z, y).
Axes of the slice: x: 2, y: 2, z: 4, core: 2. Of those that a mesh axis runs over, the one named last changes fastest.
Arguments:
- frames: bfloat16 [4, 1280, 1024], P('phase', 'seq'), may hold values from -6 to 6
- lengths: int32 [4, 8], P('phase'), may hold values from 1 to 640, 1280 in all within a row
- w_query: bfloat16 [4, 1024, 1024], P('phase', None, 'seq'), may hold values from -1 to 1
- w_key: bfloat16 [4, 1024, 1024], P('phase', None, 'seq'), may hold values from -1 to 1
- w_value: bfloat16 [4, 1024, 1024], P('phase', None, 'seq'), may hold values from -0.1875 to 0.1875
- w_output: bfloat16 [4, 1024, 1024], P('phase', None, 'seq'), may hold values from -0.1875 to 0.1875
- conv_in: bfloat16 [4, 1024, 2048], P('phase', None, 'seq'), may hold values from -0.1875 to 0.1875
- conv_taps: bfloat16 [4, 31, 1024], P('phase'), may hold values from -1 to 1
- conv_out: bfloat16 [4, 1024, 1024], P('phase', None, 'seq'), may hold values from -0.1875 to 0.1875
Outputs:
- handed: bfloat16 [4, 1280, 1024], P('phase', 'seq')
Inputs may be any that keep to these rules, and one draw needn't show every extreme that they name: Each phase's lengths sum to 1280 and the largest equals 640.
All inputs are finite; a program needn't handle non-finite values.
Results may differ from a plain program's by a relative error of at most 0.0085.
Values may be sent and summed in bfloat16 or wider, within the bound.
A program may use at most 64 MiB of HBM per device.

v0:
```python
import math
import jax
import jax.numpy as jnp
from jax import lax
from jax.sharding import PartitionSpec as P

HEADS = 16
KERNEL = 31


def padded_2(block, sides, width):
    for axis, dim in sides:
        count = lax.axis_size(axis)
        forward = [(i, i + 1) for i in range(count - 1)]
        backward = [(target, source) for source, target in forward]
        low = lax.ppermute(
            lax.slice_in_dim(block, block.shape[dim] - width, None, axis=dim), axis, forward
        )
        high = lax.ppermute(lax.slice_in_dim(block, 0, width, axis=dim), axis, backward)
        block = jnp.concatenate([low, block, high], axis=dim)
    return block


def passed_along(block, axis, distance):
    devices = range(lax.axis_size(axis))
    route = [((i - distance) % len(devices), i) for i in devices]
    return lax.ppermute(block, axis, route)


def layer_norm(values):
    centre = values - jnp.mean(values, axis=-1, keepdims=True)
    spread = jnp.mean(centre * centre, axis=-1, keepdims=True)
    return centre * lax.rsqrt(spread + 1e-05)


def segment_ids(positions, lengths):
    bounds = jnp.cumsum(lengths)
    return jnp.sum((positions[:, None] >= bounds[None, :]).astype(jnp.int32), axis=1)


def body(frames, lengths, w_query, w_key, w_value, w_output, conv_in, conv_taps, conv_out):
    hidden = frames[0]
    utt_lengths = lengths[0]
    shards = lax.axis_size("seq")
    my_index = lax.axis_index("seq")
    local_rows = hidden.shape[0]
    width = hidden.shape[1]
    total_rows = local_rows * shards
    head_size = width // HEADS
    scale = 1.0 / math.sqrt(head_size)
    groups = min(HEADS, shards)
    group_heads = HEADS // groups
    parts = shards // groups
    part_rows = local_rows // parts
    group_width = group_heads * head_size
    full_query, full_key, full_value, full_output, full_conv_in, full_conv_out = (
        lax.all_gather(w_query[0], "seq", axis=1, tiled=True),
        lax.all_gather(w_key[0], "seq", axis=1, tiled=True),
        lax.all_gather(w_value[0], "seq", axis=1, tiled=True),
        lax.all_gather(w_output[0], "seq", axis=1, tiled=True),
        lax.all_gather(conv_in[0], "seq", axis=1, tiled=True),
        lax.all_gather(conv_out[0], "seq", axis=1, tiled=True),
    )
    normed = layer_norm(hidden.astype(jnp.float32)).astype(jnp.bfloat16)
    query = jnp.dot(normed, full_query, preferred_element_type=jnp.float32).astype(jnp.bfloat16)
    key_proj = jnp.dot(normed, full_key, preferred_element_type=jnp.float32).astype(jnp.bfloat16)
    value_proj = jnp.dot(normed, full_value, preferred_element_type=jnp.float32).astype(
        jnp.bfloat16
    )
    shaped = query.reshape(parts, part_rows, groups, group_width).transpose(2, 0, 1, 3)
    query_pieces = shaped.reshape(shards, part_rows, group_width)
    kv_local = jnp.concatenate(
        [
            key_proj.reshape(local_rows, groups, group_width),
            value_proj.reshape(local_rows, groups, group_width),
        ],
        axis=2,
    )
    copies = jnp.broadcast_to(
        kv_local.transpose(1, 0, 2)[:, None], (groups, parts, local_rows, 2 * group_width)
    )
    copies = copies.reshape(shards, local_rows, 2 * group_width)
    query_got, kv_got = (
        lax.all_to_all(query_pieces, "seq", split_axis=0, concat_axis=0, tiled=True),
        lax.all_to_all(copies, "seq", split_axis=0, concat_axis=0, tiled=True),
    )
    key_value = kv_got.reshape(total_rows, 2 * group_width)
    count = shards * part_rows
    my_part = my_index % parts
    row_ids = jnp.arange(count, dtype=jnp.int32)
    query_pos = row_ids // part_rows * local_rows + my_part * part_rows + row_ids % part_rows
    queries = query_got.reshape(count, group_heads, head_size)
    key_rows = key_value[:, :group_width].reshape(total_rows, group_heads, head_size)
    value_rows = key_value[:, group_width:].reshape(total_rows, group_heads, head_size)
    seg_all = segment_ids(jnp.arange(total_rows, dtype=jnp.int32), utt_lengths)
    seg_query = segment_ids(query_pos, utt_lengths)
    query_block = math.gcd(512, count)
    blocks = count // query_block

    def attend_block(operands):
        block_query, block_seg = operands
        scores = (
            jnp.einsum("qhd,khd->hqk", block_query, key_rows, preferred_element_type=jnp.float32)
            * scale
        )
        allowed = (block_seg[:, None] == seg_all[None, :])[None]
        scores = jnp.where(allowed, scores, -1e30)
        peak = jnp.max(scores, axis=2, keepdims=True)
        expw = jnp.where(allowed, jnp.exp(scores - peak), 0.0)
        total_weight = jnp.sum(expw, axis=2)
        mixed = jnp.einsum(
            "hqk,khd->hqd",
            expw.astype(jnp.bfloat16),
            value_rows,
            preferred_element_type=jnp.float32,
        )
        mixed = mixed / total_weight[:, :, None]
        return mixed.transpose(1, 0, 2).astype(jnp.bfloat16)

    attended = lax.map(
        attend_block,
        (
            queries.reshape(blocks, query_block, group_heads, head_size),
            seg_query.reshape(blocks, query_block),
        ),
    )
    outgoing = attended.reshape(shards, part_rows, group_width)
    returned = lax.all_to_all(outgoing, "seq", split_axis=0, concat_axis=0, tiled=True)
    attended_local = (
        returned.reshape(groups, parts, part_rows, group_width)
        .transpose(1, 2, 0, 3)
        .reshape(local_rows, width)
    )
    after_attn = hidden.astype(jnp.float32) + jnp.dot(
        attended_local, full_output, preferred_element_type=jnp.float32
    )
    conv_normed = layer_norm(after_attn).astype(jnp.bfloat16)
    gates = jnp.dot(conv_normed, full_conv_in, preferred_element_type=jnp.float32)
    glu = (gates[:, :width] * jax.nn.sigmoid(gates[:, width:])).astype(jnp.bfloat16)
    reach = KERNEL // 2
    padded = padded_2(glu, (("seq", 0),), KERNEL // 2)
    padded_pos = my_index * local_rows - reach + jnp.arange(local_rows + 2 * reach, dtype=jnp.int32)
    inside = (padded_pos >= 0) & (padded_pos < total_rows)
    padded_seg = jnp.where(inside, segment_ids(padded_pos, utt_lengths), -1)
    own_seg = padded_seg[reach : reach + local_rows]
    taps = conv_taps[0]
    depthwise = jnp.zeros((local_rows, width), jnp.float32)
    for offset in range(KERNEL):
        keep = padded_seg[offset : offset + local_rows] == own_seg
        term = padded[offset : offset + local_rows].astype(jnp.float32) * taps[offset].astype(
            jnp.float32
        )
        depthwise = depthwise + jnp.where(keep[:, None], term, 0.0)
    conv_act = layer_norm(depthwise)
    conv_act = (conv_act * jax.nn.sigmoid(conv_act)).astype(jnp.bfloat16)
    block_out = (
        after_attn + jnp.dot(conv_act, full_conv_out, preferred_element_type=jnp.float32)
    ).astype(jnp.bfloat16)
    passed = passed_along(block_out, "phase", 1)
    return passed[None]


def solution(mesh):
    in_specs = (
        P("phase", "seq", None),
        P("phase", None),
        P("phase", None, "seq"),
        P("phase", None, "seq"),
        P("phase", None, "seq"),
        P("phase", None, "seq"),
        P("phase", None, "seq"),
        P("phase", None, None),
        P("phase", None, "seq"),
    )
    out_specs = P("phase", "seq", None)
    return jax.shard_map(body, mesh=mesh, in_specs=in_specs, out_specs=out_specs, check_vma=False)
```

profile of v0, /device:TPU:0, one launch (start us, length us, event | category | flops | bytes accessed | tf_op | source)
XLA Modules:
  0.0 378.4 jit_solution(5348660452825907800)
XLA Ops:
  6.5 0.7 all-gather.13.cloned.1.call-update
  7.3 0.7 all-gather.17.cloned.1.call-update
  8.1 0.7 all-gather.15.cloned.1.call-update
  8.8 0.5 all-gather.19.cloned.1.call-update
  9.4 0.5 all-gather.21.cloned.1.call-update
  9.9 1.2 convert_reduce_fusion
  11.1 1.2 fusion.77
  12.3 50.9 %all-gather.13.cloned.1.call-done = bf16[1,1024,1024]{2,1,0:T(8,128)(2,1)} async-done(((bf16[1,1024,128]{2,1,0:T(8,128)(2,1)}), bf16[1,1024,1024]{2,1,0:T(8,128)(2,1)}) %all-gather.13.cloned.1.call-update) | async-done | bytes 2097168 | tf_op jit(solution)/shard_map/all_gather | solution.py:57
  63.2 2.3 fusion.71
  65.5 0.8 copy.49
  66.3 3.4 all-to-all-start
  69.8 47.7 %all-gather.17.cloned.1.call-done = bf16[1,1024,1024]{2,1,0:T(8,128)(2,1)} async-done(((bf16[1,1024,128]{2,1,0:T(8,128)(2,1)}), bf16[1,1024,1024]{2,1,0:T(8,128)(2,1)}) %all-gather.17.cloned.1.call-update) | async-done | bytes 2097168 | tf_op jit(solution)/shard_map/all_gather | solution.py:59
  117.5 2.2 fusion.65
  119.7 49.1 %all-gather.15.cloned.1.call-done = bf16[1,1024,1024]{2,1,0:T(8,128)(2,1)} async-done(((bf16[1,1024,128]{2,1,0:T(8,128)(2,1)}), bf16[1,1024,1024]{2,1,0:T(8,128)(2,1)}) %all-gather.15.cloned.1.call-update) | async-done | bytes 2097168 | tf_op jit(solution)/shard_map/all_gather | solution.py:58
  168.8 2.1 fusion.68
  171.0 1.0 maximum_bitcast_fusion
  172.0 3.5 all-to-all-start.1
  175.6 0.5 all-gather.23.cloned.1.call-update
  176.1 0.2 reduce-window.8
  176.7 0.3 reshape_reshape.3
  177.0 1.1 copy.31
  178.2 22.7 %all-to-all-done.1 = bf16[8,160,256]{2,1,0:T(8,128)(2,1)S(1)} async-done(((bf16[8,160,256]{2,1,0:T(8,128)(2,1)}), bf16[8,160,256]{2,1,0:T(8,128)(2,1)S(1)}, u32[]{:S(2)}, u32[]{:S(2)}) %all-to-all-start.1) | async-done | bytes 655392 | tf_op jit(solution)/shard_map/all_to_all | solution.py:85
  200.9 0.9 copy.29
  201.9 0.9 copy.30
  202.8 33.4 %while.10 = (s32[]{:T(128)}, bf16[5,256,2,64]{1,3,2,0:T(8,128)(2,1)}, s32[5,256]{1,0:T(8,128)S(1)}, s32[1280]{0:T(1024)S(1)}, bf16[5,256,2,64]{1,3,2,0:T(8,128)(...) while((s32[]{:T(128)}, bf16[5,256,2,64]{1,3,2,0:T(8,128)(2,1)}, ...), condition=%wide.region_8.9_spmd, body=%wide.region_5.8_spmd.sunk | while | flops 258608128 | bytes 10696281 | solution.py:120
  202.8 0.3 broadcast_compare_fusion.2
  203.0 1.7 fusion.160
  204.7 2.4 fusion.161
  207.2 2.3 fusion.162
  209.5 0.3 broadcast_compare_fusion.2
  209.7 1.7 fusion.160
  211.4 2.4 fusion.161
  213.8 2.3 fusion.162
  216.1 0.3 broadcast_compare_fusion.2
  216.4 1.7 fusion.160
  218.1 2.4 fusion.161
  220.5 2.3 fusion.162
  222.8 0.3 broadcast_compare_fusion.2
  223.1 1.7 fusion.160
  224.7 2.4 fusion.161
  227.2 2.3 fusion.162
  229.5 0.3 broadcast_compare_fusion.2
  229.7 1.7 fusion.160
  231.4 2.4 fusion.161
  233.8 2.3 fusion.162
  236.1 1.4 copy.32
  237.5 1.0 reshape.468
  238.6 3.6 all-to-all-start.2
  242.4 15.6 %all-to-all-done.2 = bf16[8,160,128]{2,1,0:T(8,128)(2,1)S(1)} async-done(((bf16[8,160,128]{2,1,0:T(8,128)(2,1)}), bf16[8,160,128]{2,1,0:T(8,128)(2,1)S(1)}, u32[]{:S(2)}, u32[]{:S(2)}) %all-to-all-start.2) | async-done | bytes 327712 | tf_op jit(solution)/shard_map/all_to_all | solution.py:128
  258.0 0.1 copy.33
  258.2 2.2 fusion.138
  260.4 0.2 multiply_reduce_fusion.1
  260.7 50.0 %all-gather.21.cloned.1.call-done = bf16[1,1024,2048]{2,1,0:T(8,128)(2,1)} async-done(((bf16[1,1024,256]{2,1,0:T(8,128)(2,1)}), bf16[1,1024,2048]{2,1,0:T(8,128)(2,1)}) %all-gather.21.cloned.1.call-update) | async-done | bytes 4194320 | tf_op jit(solution)/shard_map/all_gather | solution.py:61
  310.7 3.1 fusion.35
  313.8 0.2 fusion.83
  314.0 3.4 collective-permute-start
  317.4 1.5 collective-permute-start.1
  319.0 4.7 %collective-permute-done.1 = bf16[15,1024]{1,0:T(8,128)(2,1)S(1)} collective-permute-done((bf16[15,1024]{1,0:T(8,128)(2,1)S(1)}, bf16[15,1024]{1,0:T(8,128)(2,1)S(1)}, u32[]{:S(2)}, u32[]{:S(2)}) %collective-permute-start.1) | collective-permute-done | bytes 30752 | tf_op jit(solution)/shard_map/ppermute | solution.py:19
  323.7 4.1 %fusion.132 = (f32[160]{0:T(256)S(1)}, f32[160,1024]{1,0:T(8,128)S(1)}) fusion(f32[1024]{0:T(1024)S(1)} %bitcast.191, bf16[15,1024]{1,0:T(8,128)(2,1)S(1)} %collective-permute-done.1, bf16[160,1024]{1,0:T(8,128)(2,1)S(1)} %fusion.83, pred[160]{0:T(512)(128)(4,1)S(1)} %get-tuple-element.146, f32[1024]{0:T(1024)S(1)} %bitcast.192, ...), kind=kLoop, calls=%fused_computation.239 | loop fusion | flops 34897760 | bytes 1176896 | tf_op jit(solution)/shard_map/reduce_sum | solution.py:31
  327.8 0.2 multiply_reduce_fusion
  328.0 34.0 %all-gather.23.cloned.1.call-done = bf16[1,1024,1024]{2,1,0:T(8,128)(2,1)} async-done(((bf16[1,1024,128]{2,1,0:T(8,128)(2,1)}), bf16[1,1024,1024]{2,1,0:T(8,128)(2,1)}) %all-gather.23.cloned.1.call-update) | async-done | bytes 2097168 | tf_op jit(solution)/shard_map/all_gather | solution.py:62
  362.0 2.2 fusion.53
  364.3 6.5 %collective-permute-done.2 = bf16[160,1024]{1,0:T(8,128)(2,1)S(1)} collective-permute-done((bf16[160,1024]{1,0:T(8,128)(2,1)S(1)}, bf16[160,1024]{1,0:T(8,128)(2,1)S(1)}, u32[]{:S(2)}, u32[]{:S(2)}) %collective-permute-start.2) | collective-permute-done | bytes 327712 | tf_op jit(solution)/shard_map/ppermute | solution.py:27
  370.8 0.7 copy.60
  (45 shorter events, 1.2 us)
Async XLA Ops:
  6.5 56.7 %all-gather.13.cloned.1.call-start = ((), (), s32[]{:S(2)}) async-start(), calls=%async_computation.3 | async-start | bytes 2359296 | tf_op jit(solution)/shard_map/all_gather | solution.py:57
  7.3 110.2 %all-gather.17.cloned.1.call-start = ((), (), s32[]{:S(2)}) async-start(), calls=%async_computation.5 | async-start | bytes 2359296 | tf_op jit(solution)/shard_map/all_gather | solution.py:59
  8.0 160.8 %all-gather.15.cloned.1.call-start = ((), (), s32[]{:S(2)}) async-start(), calls=%async_computation.4 | async-start | bytes 2359296 | tf_op jit(solution)/shard_map/all_gather | solution.py:58
  8.7 249.5 %all-gather.19.cloned.1.call-start = ((), (), s32[]{:S(2)}) async-start(), calls=%async_computation.6 | async-start | bytes 2359296 | tf_op jit(solution)/shard_map/all_gather | solution.py:60
  9.3 301.4 %all-gather.21.cloned.1.call-start = ((), (), s32[]{:S(2)}) async-start(), calls=%async_computation.7 | async-start | bytes 4718592 | tf_op jit(solution)/shard_map/all_gather | solution.py:61
  9.9 107.6 %copy-start = (bf16[1,160,1024]{2,1,0:T(8,128)(2,1)S(1)}, bf16[1,160,1024]{2,1,0:T(8,128)(2,1)}, u32[]{:S(2)}) copy-start(bf16[1,160,1024]{2,1,0:T(8,128)(2,1)} %param.11) | copy-start | bytes 983044
  66.3 105.7 %all-to-all-start = ((bf16[8,160,128]{2,1,0:T(8,128)(2,1)}), bf16[8,160,128]{2,1,0:T(8,128)(2,1)S(1)}, u32[]{:S(2)}, u32[]{:S(2)}) async-start(bf16[8,160,128]{2,1,0:T(8,128)(2,1)} %bitcast.150), calls=%async_computation | async-start | bytes 655360 | tf_op jit(solution)/shard_map/all_to_all | solution.py:84
  119.7 56.4 %copy-start.2 = (s32[1,8]{1,0:T(1,128)S(1)}, s32[1,8]{1,0:T(1,128)}, u32[]{:S(2)}) copy-start(s32[1,8]{1,0:T(1,128)} %param.12) | copy-start | bytes 100
  119.7 57.0 %copy-start.1 = (bf16[1,31,1024]{2,1,0:T(8,128)(2,1)S(1)}, bf16[1,31,1024]{2,1,0:T(8,128)(2,1)}, u32[]{:S(2)}) copy-start(bf16[1,31,1024]{2,1,0:T(8,128)(2,1)} %param.18) | copy-start | bytes 190468
  172.0 28.9 %all-to-all-start.1 = ((bf16[8,160,256]{2,1,0:T(8,128)(2,1)}), bf16[8,160,256]{2,1,0:T(8,128)(2,1)S(1)}, u32[]{:S(2)}, u32[]{:S(2)}) async-start(bf16[8,160,256]{2,1,0:T(8,128)(2,1)} %maximum_bitcast_fusion), calls=%async_computation.1 | async-start | bytes 1310720 | tf_op jit(solution)/shard_map/all_to_all | solution.py:85
  175.5 186.5 %all-gather.23.cloned.1.call-start = ((), (), s32[]{:S(2)}) async-start(), calls=%async_computation.8 | async-start | bytes 2359296 | tf_op jit(solution)/shard_map/all_gather | solution.py:62
  238.6 19.5 %all-to-all-start.2 = ((bf16[8,160,128]{2,1,0:T(8,128)(2,1)}), bf16[8,160,128]{2,1,0:T(8,128)(2,1)S(1)}, u32[]{:S(2)}, u32[]{:S(2)}) async-start(bf16[8,160,128]{2,1,0:T(8,128)(2,1)} %reshape.468), calls=%async_computation.2 | async-start | bytes 655360 | tf_op jit(solution)/shard_map/all_to_all | solution.py:128
  314.0 5.0 %collective-permute-start = (bf16[15,1024]{1,0:T(8,128)(2,1)S(1)}, bf16[15,1024]{1,0:T(8,128)(2,1)S(1)}, u32[]{:S(2)}, u32[]{:S(2)}) collective-permute-start(bf16[15,1024]{1,0:T(8,128)(2,1)S(1)} %get-tuple-element.84), channel_id=1, source_target_pairs={{0,1},{1,2},{2,3},{3,4},{4,5},{5,6},{6,7},{8,9},{9,10},{10,11},{11... | collective-permute-start | bytes 92168 | tf_op jit(solution)/shard_map/ppermute | solution.py:16
  317.4 6.3 %collective-permute-start.1 = (bf16[15,1024]{1,0:T(8,128)(2,1)S(1)}, bf16[15,1024]{1,0:T(8,128)(2,1)S(1)}, u32[]{:S(2)}, u32[]{:S(2)}) collective-permute-start(bf16[15,1024]{1,0:T(8,128)(2,1)S(1)} %get-tuple-element.85), channel_id=1, source_target_pairs={{1,0},{2,1},{3,2},{4,3},{5,4},{6,5},{7,6},{9,8},{10,9},{11,10},{12... | collective-permute-start | bytes 92168 | tf_op jit(solution)/shard_map/ppermute | solution.py:19
  364.2 6.6 %collective-permute-start.2 = (bf16[160,1024]{1,0:T(8,128)(2,1)S(1)}, bf16[160,1024]{1,0:T(8,128)(2,1)S(1)}, u32[]{:S(2)}, u32[]{:S(2)}) collective-permute-start(bf16[160,1024]{1,0:T(8,128)(2,1)S(1)} %fusion.53), channel_id=1, source_target_pairs={{24,0},{0,8},{8,16},{16,24},{25,1},{1,9},{9,17},{17,25},{26,2},{2,... | collective-permute-start | bytes 983048 | tf_op jit(solution)/shard_map/ppermute | solution.py:27
Sparse Core Ops, SparseCore 0:
  9.4 53.7 all-gather.12
  65.2 52.1 all-gather.16
  119.5 49.2 all-gather.14
  170.7 57.7 all-gather.18
  230.4 80.2 all-gather.20
  312.6 49.3 all-gather.22
where the time goes:
time: 379 us; the launch traced here: 378 us
  waiting for transfers between devices  285 us (75%)
  matrix products  46 us (12%)
  starting transfers between devices  15.7 us (4%)
  between operations  13.8 us (4%)
  other arithmetic  10.2 us (3%)
  local copies, waits for them, and re-layouts  7.62 us (2%)
    all_gather x1, waiting for transfers between devices, body(): lax.all_gather(w_query[0], 'seq', axis=1, tiled=True)  50.9 us
    all_gather x1, waiting for transfers between devices, body(): lax.all_gather(conv_in[0], 'seq', axis=1, tiled=True)  50 us
    all_gather x1, waiting for transfers between devices, body(): lax.all_gather(w_key[0], 'seq', axis=1, tiled=True)  49.1 us
    all_gather x1, waiting for transfers between devices, body(): lax.all_gather(w_value[0], 'seq', axis=1, tiled=True)  47.7 us
    all_gather x1, waiting for transfers between devices, body(): lax.all_gather(conv_out[0], 'seq', axis=1, tiled=True)  34 us
    all_to_all x1, waiting for transfers between devices, body(): lax.all_to_all(copies, 'seq', split_axis=0, concat_axis=0, tiled=True)  22.7 us
    all_to_all x1, waiting for transfers between devices, body(): lax.all_to_all(outgoing, 'seq', split_axis=0, concat_axis=0, tiled=True)  15.6 us
    sub x5, matrix products, attend_block(): expw = jnp.where(allowed, jnp.exp(scores - peak), 0.0)  12.2 us
  transfers between devices with their start and end apart: 12, of which 9 were waited for; matrix products, arithmetic and copies ran while one was open for 16% of the time, Pallas kernels for 0%

commit v1 on v0

--- a/solution.py
+++ b/solution.py
@@ -6,6 +6,27 @@
 
 HEADS = 16
 KERNEL = 31
+
+
+def gather_around(value, axis, dim):
+    devices, position, width = (lax.axis_size(axis), lax.axis_index(axis), value.shape[dim])
+    upward = [(i, (i + 1) % devices) for i in range(devices)]
+    behind = [(i, (i - 1) % devices) for i in range(devices)]
+    result = jnp.zeros((*value.shape[:dim], devices * width, *value.shape[dim + 1 :]), value.dtype)
+    result = lax.dynamic_update_slice_in_dim(result, value, position * width, axis=dim)
+    from_left = from_right = value
+    halfway = devices // 2
+    for turn in range(1, halfway + 1):
+        from_left = lax.ppermute(from_left, axis, upward)
+        result = lax.dynamic_update_slice_in_dim(
+            result, from_left, (position - turn) % devices * width, axis=dim
+        )
+        if turn < devices - halfway:
+            from_right = lax.ppermute(from_right, axis, behind)
+            result = lax.dynamic_update_slice_in_dim(
+                result, from_right, (position + turn) % devices * width, axis=dim
+            )
+    return result
 
 
 def padded_2(block, sides, width):
@@ -56,7 +77,7 @@
     full_query, full_key, full_value, full_output, full_conv_in, full_conv_out = (
         lax.all_gather(w_query[0], "seq", axis=1, tiled=True),
         lax.all_gather(w_key[0], "seq", axis=1, tiled=True),
-        lax.all_gather(w_value[0], "seq", axis=1, tiled=True),
+        gather_around(w_value[0], "seq", 1),
         lax.all_gather(w_output[0], "seq", axis=1, tiled=True),
         lax.all_gather(conv_in[0], "seq", axis=1, tiled=True),
         lax.all_gather(conv_out[0], "seq", axis=1, tiled=True),

time: 379 us -> 347 us (0.916)
  waiting for transfers between devices: 285 us -> 238 us
  starting transfers between devices: 15.7 us -> 34 us
    all_gather x1 -> x0, waiting for transfers between devices: 47.7 us -> none  [body(): lax.all_gather(w_value[0], 'seq', axis=1, tiled=True)]
    ppermute x0 -> x7, waiting for transfers between devices: none -> 35.1 us  [the longest x4 25.8 us: gather_around(): from_left = lax.ppermute(from_left, axis, upward)]
    all_gather x1, waiting for transfers between devices: 50.9 us -> 16.8 us  [body(): lax.all_gather(w_query[0], 'seq', axis=1, tiled=True)]
    ppermute x0 -> x7, starting transfers between devices: none -> 17.9 us  [the longest x3 12.5 us: gather_around(): from_right = lax.ppermute(from_right, axis, behind)]
  transfers between devices with their start and end apart: 12 -> 18, of which waited for: 9 -> 14; matrix products, arithmetic and copies ran while one was open for 16% -> 17% of each run, Pallas kernels for 0% -> 0%
where the time goes in v1:
time: 347 us; the launch traced here: 346 us
  waiting for transfers between devices  238 us (69%)
  matrix products  44.4 us (13%)
  starting transfers between devices  34 us (10%)
  between operations  13.5 us (4%)
  local copies, waits for them, and re-layouts  8.57 us (2%)
  other arithmetic  8.13 us (2%)
    all_gather x1, waiting for transfers between devices, body(): lax.all_gather(conv_in[0], 'seq', axis=1, tiled=True)  50 us
    all_gather x1, waiting for transfers between devices, body(): lax.all_gather(w_key[0], 'seq', axis=1, tiled=True)  49.2 us
    all_gather x1, waiting for transfers between devices, body(): lax.all_gather(conv_out[0], 'seq', axis=1, tiled=True)  34 us
    ppermute x4, waiting for transfers between devices, gather_around(): from_left = lax.ppermute(from_left, axis, upward)  25.8 us
    all_to_all x1, waiting for transfers between devices, body(): lax.all_to_all(copies, 'seq', split_axis=0, concat_axis=0, tiled=True)  22.7 us
    all_gather x1, waiting for transfers between devices, body(): lax.all_gather(w_query[0], 'seq', axis=1, tiled=True)  16.8 us
    all_to_all x1, waiting for transfers between devices, body(): lax.all_to_all(outgoing, 'seq', split_axis=0, concat_axis=0, tiled=True)  15.6 us
    ppermute x3, starting transfers between devices, gather_around(): from_right = lax.ppermute(from_right, axis, behind)  12.5 us
  transfers between devices with their start and end apart: 18, of which 14 were waited for; matrix products, arithmetic and copies ran while one was open for 17% of the time, Pallas kernels for 0%

profile of v1, /device:TPU:0, one launch (start us, length us, event | category | flops | bytes accessed | tf_op | source)
XLA Modules:
  0.0 346.5 jit_solution(13856027414334923147)
XLA Ops:
  6.5 0.7 all-gather.11.cloned.1.call-update
  7.3 0.7 all-gather.13.cloned.1.call-update
  8.1 0.7 all-gather.15.cloned.1.call-update
  8.8 0.5 all-gather.17.cloned.1.call-update
  9.3 3.0 collective-permute-start
  12.3 3.1 collective-permute-start.1
  16.0 10.7 %collective-permute-done = bf16[1024,128]{1,0:T(8,128)(2,1)S(1)} collective-permute-done((bf16[1024,128]{1,0:T(8,128)(2,1)}, bf16[1024,128]{1,0:T(8,128)(2,1)S(1)}, u32[]{:S(2)}, u32[]{:S(2)}) %collective-permute-start) | collective-permute-done | bytes 262176 | tf_op jit(solution)/shard_map/ppermute | solution.py:20
  26.6 2.4 collective-permute-start.2
  29.3 3.8 %collective-permute-start.3 = (bf16[1024,128]{1,0:T(8,128)(2,1)S(1)}, bf16[1024,128]{1,0:T(8,128)(2,1)S(1)}, u32[]{:S(2)}, u32[]{:S(2)}) collective-permute-start(bf16[1024,128]{1,0:T(8,128)(2,1)S(1)} %collective-permute-done.1), channel_id=1, source_target_pairs={{0,7},{1,0},{2,1},{3,2},{4,3},{5,4},{6,5},{7,6},{8,15},{9,8},{10,9... | collective-permute-start | bytes 786440 | tf_op jit(solution)/shard_map/ppermute | solution.py:25
  33.1 7.6 %collective-permute-done.2 = bf16[1024,128]{1,0:T(8,128)(2,1)S(1)} collective-permute-done((bf16[1024,128]{1,0:T(8,128)(2,1)S(1)}, bf16[1024,128]{1,0:T(8,128)(2,1)S(1)}, u32[]{:S(2)}, u32[]{:S(2)}) %collective-permute-start.2) | collective-permute-done | bytes 262176 | tf_op jit(solution)/shard_map/ppermute | solution.py:20
  40.9 0.4 collective-permute-done.3
  41.3 5.6 %collective-permute-start.5 = (bf16[1024,128]{1,0:T(8,128)(2,1)S(1)}, bf16[1024,128]{1,0:T(8,128)(2,1)S(1)}, u32[]{:S(2)}, u32[]{:S(2)}) collective-permute-start(bf16[1024,128]{1,0:T(8,128)(2,1)S(1)} %collective-permute-done.3), channel_id=1, source_target_pairs={{0,7},{1,0},{2,1},{3,2},{4,3},{5,4},{6,5},{7,6},{8,15},{9,8},{10,9... | collective-permute-start | bytes 786440 | tf_op jit(solution)/shard_map/ppermute | solution.py:25
  47.0 2.9 collective-permute-done.4
  50.1 8.9 %collective-permute-done.5 = bf16[1024,128]{1,0:T(8,128)(2,1)S(1)} collective-permute-done((bf16[1024,128]{1,0:T(8,128)(2,1)S(1)}, bf16[1024,128]{1,0:T(8,128)(2,1)S(1)}, u32[]{:S(2)}, u32[]{:S(2)}) %collective-permute-start.5) | collective-permute-done | bytes 262176 | tf_op jit(solution)/shard_map/ppermute | solution.py:25
  59.1 4.6 %collective-permute-done.6 = bf16[1024,128]{1,0:T(8,128)(2,1)S(1)} collective-permute-done((bf16[1024,128]{1,0:T(8,128)(2,1)S(1)}, bf16[1024,128]{1,0:T(8,128)(2,1)S(1)}, u32[]{:S(2)}, u32[]{:S(2)}) %collective-permute-start.6) | collective-permute-done | bytes 262176 | tf_op jit(solution)/shard_map/ppermute | solution.py:20
  63.8 16.8 %all-gather.11.cloned.1.call-done = bf16[1,1024,1024]{2,1,0:T(8,128)(2,1)} async-done(((bf16[1,1024,128]{2,1,0:T(8,128)(2,1)}), bf16[1,1024,1024]{2,1,0:T(8,128)(2,1)}) %all-gather.11.cloned.1.call-update) | async-done | bytes 2097168 | tf_op jit(solution)/shard_map/all_gather | solution.py:78
  80.6 2.1 fusion.64
  82.8 0.8 copy.49
  83.5 3.9 %all-to-all-start = ((bf16[8,160,128]{2,1,0:T(8,128)(2,1)}), bf16[8,160,128]{2,1,0:T(8,128)(2,1)S(1)}, u32[]{:S(2)}, u32[]{:S(2)}) async-start(bf16[8,160,128]{2,1,0:T(8,128)(2,1)} %bitcast.146), calls=%async_computation | async-start | bytes 655360 | tf_op jit(solution)/shard_map/all_to_all | solution.py:105
  87.4 0.6 fusion.60
  88.0 49.2 %all-gather.13.cloned.1.call-done = bf16[1,1024,1024]{2,1,0:T(8,128)(2,1)} async-done(((bf16[1,1024,128]{2,1,0:T(8,128)(2,1)}), bf16[1,1024,1024]{2,1,0:T(8,128)(2,1)}) %all-gather.13.cloned.1.call-update) | async-done | bytes 2097168 | tf_op jit(solution)/shard_map/all_gather | solution.py:79
  137.2 2.2 fusion.61
  139.5 1.0 maximum_bitcast_fusion
  140.4 3.5 %all-to-all-start.1 = ((bf16[8,160,256]{2,1,0:T(8,128)(2,1)}), bf16[8,160,256]{2,1,0:T(8,128)(2,1)S(1)}, u32[]{:S(2)}, u32[]{:S(2)}) async-start(bf16[8,160,256]{2,1,0:T(8,128)(2,1)} %maximum_bitcast_fusion), calls=%async_computation.1 | async-start | bytes 1310720 | tf_op jit(solution)/shard_map/all_to_all | solution.py:106
  144.0 0.5 all-gather.19.cloned.1.call-update
  145.2 0.3 reshape_reshape.3
  145.5 1.1 copy.31
  146.6 22.7 %all-to-all-done.1 = bf16[8,160,256]{2,1,0:T(8,128)(2,1)S(1)} async-done(((bf16[8,160,256]{2,1,0:T(8,128)(2,1)}), bf16[8,160,256]{2,1,0:T(8,128)(2,1)S(1)}, u32[]{:S(2)}, u32[]{:S(2)}) %all-to-all-start.1) | async-done | bytes 655392 | tf_op jit(solution)/shard_map/all_to_all | solution.py:106
  169.3 1.0 copy.29
  170.3 0.9 copy.30
  171.2 33.4 %while.10 = (s32[]{:T(128)}, bf16[5,256,2,64]{1,3,2,0:T(8,128)(2,1)}, s32[5,256]{1,0:T(8,128)S(1)}, s32[1280]{0:T(1024)S(1)}, bf16[5,256,2,64]{1,3,2,0:T(8,128)(...) while((s32[]{:T(128)}, bf16[5,256,2,64]{1,3,2,0:T(8,128)(2,1)}, ...), condition=%wide.region_8.9_spmd, body=%wide.region_5.8_spmd.sunk | while | flops 258608128 | bytes 10696281 | solution.py:141
  171.2 0.3 broadcast_compare_fusion.2
  171.5 1.7 fusion.154
  173.2 2.4 fusion.155
  175.6 2.3 fusion.156
  177.9 0.3 broadcast_compare_fusion.2
  178.2 1.7 fusion.154
  179.9 2.4 fusion.155
  182.3 2.3 fusion.156
  184.6 0.3 broadcast_compare_fusion.2
  184.9 1.7 fusion.154
  186.5 2.4 fusion.155
  189.0 2.3 fusion.156
  191.5 1.7 fusion.154
  193.2 2.4 fusion.155
  195.6 2.3 fusion.156
  198.2 1.7 fusion.154
  199.9 2.4 fusion.155
  202.3 2.3 fusion.156
  204.6 1.4 copy.32
  206.0 1.0 reshape.468
  207.0 3.6 %all-to-all-start.2 = ((bf16[8,160,128]{2,1,0:T(8,128)(2,1)}), bf16[8,160,128]{2,1,0:T(8,128)(2,1)S(1)}, u32[]{:S(2)}, u32[]{:S(2)}) async-start(bf16[8,160,128]{2,1,0:T(8,128)(2,1)} %reshape.468), calls=%async_computation.2 | async-start | bytes 655360 | tf_op jit(solution)/shard_map/all_to_all | solution.py:149
  210.9 15.6 %all-to-all-done.2 = bf16[8,160,128]{2,1,0:T(8,128)(2,1)S(1)} async-done(((bf16[8,160,128]{2,1,0:T(8,128)(2,1)}), bf16[8,160,128]{2,1,0:T(8,128)(2,1)S(1)}, u32[]{:S(2)}, u32[]{:S(2)}) %all-to-all-start.2) | async-done | bytes 327712 | tf_op jit(solution)/shard_map/all_to_all | solution.py:149
  226.7 2.2 fusion.131
  229.1 50.0 %all-gather.17.cloned.1.call-done = bf16[1,1024,2048]{2,1,0:T(8,128)(2,1)} async-done(((bf16[1,1024,256]{2,1,0:T(8,128)(2,1)}), bf16[1,1024,2048]{2,1,0:T(8,128)(2,1)}) %all-gather.17.cloned.1.call-update) | async-done | bytes 4194320 | tf_op jit(solution)/shard_map/all_gather | solution.py:82
  279.2 3.1 fusion.35
  282.5 3.4 collective-permute-start.7
  285.8 1.5 collective-permute-start.8
  287.4 4.7 %collective-permute-done.8 = bf16[15,1024]{1,0:T(8,128)(2,1)S(1)} collective-permute-done((bf16[15,1024]{1,0:T(8,128)(2,1)S(1)}, bf16[15,1024]{1,0:T(8,128)(2,1)S(1)}, u32[]{:S(2)}, u32[]{:S(2)}) %collective-permute-start.8) | collective-permute-done | bytes 30752 | tf_op jit(solution)/shard_map/ppermute | solution.py:40
  292.1 4.1 %fusion.125 = (f32[160]{0:T(256)S(1)}, f32[160,1024]{1,0:T(8,128)S(1)}) fusion(f32[1024]{0:T(1024)S(1)} %bitcast.189, bf16[15,1024]{1,0:T(8,128)(2,1)S(1)} %collective-permute-done.8, bf16[160,1024]{1,0:T(8,128)(2,1)S(1)} %fusion.76, pred[160]{0:T(512)(128)(4,1)S(1)} %get-tuple-element.146, f32[1024]{0:T(1024)S(1)} %bitcast.190, ...), kind=kLoop, calls=%fused_computation.245 | loop fusion | flops 34897760 | bytes 1176896 | tf_op jit(solution)/shard_map/reduce_sum | solution.py:52
  296.5 34.0 %all-gather.19.cloned.1.call-done = bf16[1,1024,1024]{2,1,0:T(8,128)(2,1)} async-done(((bf16[1,1024,128]{2,1,0:T(8,128)(2,1)}), bf16[1,1024,1024]{2,1,0:T(8,128)(2,1)}) %all-gather.19.cloned.1.call-update) | async-done | bytes 2097168 | tf_op jit(solution)/shard_map/all_gather | solution.py:83
  330.5 2.2 fusion.51
  332.7 6.5 %collective-permute-done.9 = bf16[160,1024]{1,0:T(8,128)(2,1)S(1)} collective-permute-done((bf16[160,1024]{1,0:T(8,128)(2,1)S(1)}, bf16[160,1024]{1,0:T(8,128)(2,1)S(1)}, u32[]{:S(2)}, u32[]{:S(2)}) %collective-permute-start.9) | collective-permute-done | bytes 327712 | tf_op jit(solution)/shard_map/ppermute | solution.py:48
  339.2 0.7 copy.68
  (67 shorter events, 3.9 us)
Async XLA Ops:
  6.5 9.2 %copy-start.1 = (bf16[1,1024,128]{2,1,0:T(8,128)(2,1)S(1)}, bf16[1,1024,128]{2,1,0:T(8,128)(2,1)}, u32[]{:S(2)}) copy-start(bf16[1,1024,128]{2,1,0:T(8,128)(2,1)} %param.15) | copy-start | bytes 786436
  6.5 9.3 %copy-start = (bf16[1,160,1024]{2,1,0:T(8,128)(2,1)S(1)}, bf16[1,160,1024]{2,1,0:T(8,128)(2,1)}, u32[]{:S(2)}) copy-start(bf16[1,160,1024]{2,1,0:T(8,128)(2,1)} %param.11) | copy-start | bytes 983044
  6.5 74.0 %all-gather.11.cloned.1.call-start = ((), (), s32[]{:S(2)}) async-start(), calls=%async_computation.3 | async-start | bytes 2359296 | tf_op jit(solution)/shard_map/all_gather | solution.py:78
  7.3 130.0 %all-gather.13.cloned.1.call-start = ((), (), s32[]{:S(2)}) async-start(), calls=%async_computation.4 | async-start | bytes 2359296 | tf_op jit(solution)/shard_map/all_gather | solution.py:79
  8.0 218.7 %all-gather.15.cloned.1.call-start = ((), (), s32[]{:S(2)}) async-start(), calls=%async_computation.5 | async-start | bytes 2359296 | tf_op jit(solution)/shard_map/all_gather | solution.py:81
  8.7 270.4 %all-gather.17.cloned.1.call-start = ((), (), s32[]{:S(2)}) async-start(), calls=%async_computation.6 | async-start | bytes 4718592 | tf_op jit(solution)/shard_map/all_gather | solution.py:82
  9.3 17.3 %collective-permute-start = (bf16[1024,128]{1,0:T(8,128)(2,1)}, bf16[1024,128]{1,0:T(8,128)(2,1)S(1)}, u32[]{:S(2)}, u32[]{:S(2)}) collective-permute-start(bf16[1024,128]{1,0:T(8,128)(2,1)} %bitcast.176), channel_id=1, source_target_pairs={{0,1},{1,2},{2,3},{3,4},{4,5},{5,6},{6,7},{7,0},{8,9},{9,10},{10,1... | collective-permute-start | bytes 786440 | tf_op jit(solution)/shard_map/ppermute | solution.py:20
  12.3 16.9 %collective-permute-start.1 = (bf16[1024,128]{1,0:T(8,128)(2,1)}, bf16[1024,128]{1,0:T(8,128)(2,1)S(1)}, u32[]{:S(2)}, u32[]{:S(2)}) collective-permute-start(bf16[1024,128]{1,0:T(8,128)(2,1)} %bitcast.177), channel_id=1, source_target_pairs={{0,7},{1,0},{2,1},{3,2},{4,3},{5,4},{6,5},{7,6},{8,15},{9,8},{10,9... | collective-permute-start | bytes 786440 | tf_op jit(solution)/shard_map/ppermute | solution.py:25
  26.6 14.0 %collective-permute-start.2 = (bf16[1024,128]{1,0:T(8,128)(2,1)S(1)}, bf16[1024,128]{1,0:T(8,128)(2,1)S(1)}, u32[]{:S(2)}, u32[]{:S(2)}) collective-permute-start(bf16[1024,128]{1,0:T(8,128)(2,1)S(1)} %collective-permute-done), channel_id=1, source_target_pairs={{0,1},{1,2},{2,3},{3,4},{4,5},{5,6},{6,7},{7,0},{8,9},{9,10},{10,1... | collective-permute-start | bytes 786440 | tf_op jit(solution)/shard_map/ppermute | solution.py:20
  29.3 12.0 %collective-permute-start.3 = (bf16[1024,128]{1,0:T(8,128)(2,1)S(1)}, bf16[1024,128]{1,0:T(8,128)(2,1)S(1)}, u32[]{:S(2)}, u32[]{:S(2)}) collective-permute-start(bf16[1024,128]{1,0:T(8,128)(2,1)S(1)} %collective-permute-done.1), channel_id=1, source_target_pairs={{0,7},{1,0},{2,1},{3,2},{4,3},{5,4},{6,5},{7,6},{8,15},{9,8},{10,9... | collective-permute-start | bytes 786440 | tf_op jit(solution)/shard_map/ppermute | solution.py:25
  40.7 9.2 %collective-permute-start.4 = (bf16[1024,128]{1,0:T(8,128)(2,1)S(1)}, bf16[1024,128]{1,0:T(8,128)(2,1)S(1)}, u32[]{:S(2)}, u32[]{:S(2)}) collective-permute-start(bf16[1024,128]{1,0:T(8,128)(2,1)S(1)} %collective-permute-done.2), channel_id=1, source_target_pairs={{0,1},{1,2},{2,3},{3,4},{4,5},{5,6},{6,7},{7,0},{8,9},{9,10},{10,1... | collective-permute-start | bytes 786440 | tf_op jit(solution)/shard_map/ppermute | solution.py:20
  41.3 17.7 %collective-permute-start.5 = (bf16[1024,128]{1,0:T(8,128)(2,1)S(1)}, bf16[1024,128]{1,0:T(8,128)(2,1)S(1)}, u32[]{:S(2)}, u32[]{:S(2)}) collective-permute-start(bf16[1024,128]{1,0:T(8,128)(2,1)S(1)} %collective-permute-done.3), channel_id=1, source_target_pairs={{0,7},{1,0},{2,1},{3,2},{4,3},{5,4},{6,5},{7,6},{8,15},{9,8},{10,9... | collective-permute-start | bytes 786440 | tf_op jit(solution)/shard_map/ppermute | solution.py:25
  49.9 13.8 %collective-permute-start.6 = (bf16[1024,128]{1,0:T(8,128)(2,1)S(1)}, bf16[1024,128]{1,0:T(8,128)(2,1)S(1)}, u32[]{:S(2)}, u32[]{:S(2)}) collective-permute-start(bf16[1024,128]{1,0:T(8,128)(2,1)S(1)} %collective-permute-done.4), channel_id=1, source_target_pairs={{0,1},{1,2},{2,3},{3,4},{4,5},{5,6},{6,7},{7,0},{8,9},{9,10},{10,1... | collective-permute-start | bytes 786440 | tf_op jit(solution)/shard_map/ppermute | solution.py:20
  83.5 56.9 %all-to-all-start = ((bf16[8,160,128]{2,1,0:T(8,128)(2,1)}), bf16[8,160,128]{2,1,0:T(8,128)(2,1)S(1)}, u32[]{:S(2)}, u32[]{:S(2)}) async-start(bf16[8,160,128]{2,1,0:T(8,128)(2,1)} %bitcast.146), calls=%async_computation | async-start | bytes 655360 | tf_op jit(solution)/shard_map/all_to_all | solution.py:105
  139.4 5.2 %copy-start.3 = (s32[1,8]{1,0:T(1,128)S(1)}, s32[1,8]{1,0:T(1,128)}, u32[]{:S(2)}) copy-start(s32[1,8]{1,0:T(1,128)} %param.12) | copy-start | bytes 100
  139.4 5.7 %copy-start.2 = (bf16[1,31,1024]{2,1,0:T(8,128)(2,1)S(1)}, bf16[1,31,1024]{2,1,0:T(8,128)(2,1)}, u32[]{:S(2)}) copy-start(bf16[1,31,1024]{2,1,0:T(8,128)(2,1)} %param.18) | copy-start | bytes 190468
  140.4 28.9 %all-to-all-start.1 = ((bf16[8,160,256]{2,1,0:T(8,128)(2,1)}), bf16[8,160,256]{2,1,0:T(8,128)(2,1)S(1)}, u32[]{:S(2)}, u32[]{:S(2)}) async-start(bf16[8,160,256]{2,1,0:T(8,128)(2,1)} %maximum_bitcast_fusion), calls=%async_computation.1 | async-start | bytes 1310720 | tf_op jit(solution)/shard_map/all_to_all | solution.py:106
  144.0 186.5 %all-gather.19.cloned.1.call-start = ((), (), s32[]{:S(2)}) async-start(), calls=%async_computation.7 | async-start | bytes 2359296 | tf_op jit(solution)/shard_map/all_gather | solution.py:83
  207.0 19.5 %all-to-all-start.2 = ((bf16[8,160,128]{2,1,0:T(8,128)(2,1)}), bf16[8,160,128]{2,1,0:T(8,128)(2,1)S(1)}, u32[]{:S(2)}, u32[]{:S(2)}) async-start(bf16[8,160,128]{2,1,0:T(8,128)(2,1)} %reshape.468), calls=%async_computation.2 | async-start | bytes 655360 | tf_op jit(solution)/shard_map/all_to_all | solution.py:149
  282.5 4.9 %collective-permute-start.7 = (bf16[15,1024]{1,0:T(8,128)(2,1)S(1)}, bf16[15,1024]{1,0:T(8,128)(2,1)S(1)}, u32[]{:S(2)}, u32[]{:S(2)}) collective-permute-start(bf16[15,1024]{1,0:T(8,128)(2,1)S(1)} %get-tuple-element.84), channel_id=1, source_target_pairs={{0,1},{1,2},{2,3},{3,4},{4,5},{5,6},{6,7},{8,9},{9,10},{10,11},{11... | collective-permute-start | bytes 92168 | tf_op jit(solution)/shard_map/ppermute | solution.py:37
  285.8 6.3 %collective-permute-start.8 = (bf16[15,1024]{1,0:T(8,128)(2,1)S(1)}, bf16[15,1024]{1,0:T(8,128)(2,1)S(1)}, u32[]{:S(2)}, u32[]{:S(2)}) collective-permute-start(bf16[15,1024]{1,0:T(8,128)(2,1)S(1)} %get-tuple-element.85), channel_id=1, source_target_pairs={{1,0},{2,1},{3,2},{4,3},{5,4},{6,5},{7,6},{9,8},{10,9},{11,10},{12... | collective-permute-start | bytes 92168 | tf_op jit(solution)/shard_map/ppermute | solution.py:40
  332.7 6.6 %collective-permute-start.9 = (bf16[160,1024]{1,0:T(8,128)(2,1)S(1)}, bf16[160,1024]{1,0:T(8,128)(2,1)S(1)}, u32[]{:S(2)}, u32[]{:S(2)}) collective-permute-start(bf16[160,1024]{1,0:T(8,128)(2,1)S(1)} %fusion.51), channel_id=1, source_target_pairs={{24,0},{0,8},{8,16},{16,24},{25,1},{1,9},{9,17},{17,25},{26,2},{2,... | collective-permute-start | bytes 983048 | tf_op jit(solution)/shard_map/ppermute | solution.py:48
Sparse Core Ops, SparseCore 0:
  9.4 71.0 all-gather.10
  82.6 54.5 all-gather.12
  139.3 57.6 all-gather.14
  198.8 80.2 all-gather.16
  281.1 49.3 all-gather.18
